TPU v7x, 128 devices: a whole 4x4x4 slice. The times are simulated.
128 devices in a mesh: pipe: 2 (over x_hi), ctx: 8 (over x_lo, z), tp: 8 (over y, core).
Axes of the slice: x: 4 (x_hi: 2, x_lo: 2; x = x_hi * 2 + x_lo), y: 4, z: 4, core: 2. Of those that a mesh axis runs over, the one named last changes fastest.
Arguments:
- queries: bfloat16 [2, 2, 4096, 8192], P('pipe', None, 'ctx', 'tp'), may hold values from -220 to 220
- keys: bfloat16 [2, 2, 4096, 1024], P('pipe', None, 'ctx', 'tp'), may hold values from -8 to 8
- values: bfloat16 [2, 2, 4096, 1024], P('pipe', None, 'ctx', 'tp'), may hold values from -16 to 16
- doc_start: int32 [2, 4096], P(None, 'ctx'), may hold values from 0 to 4095, as said below
- owners: int32 [2, 128], P(None, 'ctx'), may hold values from 0 to 7, as said below
Outputs:
- balanced: bfloat16 [2, 2, 8, 8, 3, 32, 8192], P('pipe', None, 'ctx', None, None, None, 'tp')
Inputs may be any that keep to these rules, and one draw needn't show every extreme that they name: doc_start[m, i] is the first token of token i's document: it never decreases along the slab, is at most i, i - doc_start[m, i] < 256, and every slab holds a document of exactly 256 tokens. `owners`: of the 16 tracts that lie on one index of ctx, at most 3 have the same owner, and in every such block some owner gets exactly 3.
All inputs are finite; a program needn't handle non-finite values.
Results may differ from a plain program's by a relative error of at most 0.0063.
Values may be sent and summed in bfloat16 or wider, within the bound.
A program may use at most 128 MiB of HBM per device.

v0:
```python
import math
import jax
import jax.numpy as jnp
from jax import lax
from jax.sharding import PartitionSpec as P

HEAD_WIDTH = 128
TRACTS_DEV = 16
DOCMAX = 256


def shifted(block, axis, distance):
    devices = range(lax.axis_size(axis))
    route = [(i - distance, i) for i in devices if i - distance in devices]
    return lax.ppermute(block, axis, route)


def rank_table(owner_list, owner_count, slot_count):
    tract_count = owner_list.shape[0]
    positions = jnp.arange(tract_count, dtype=jnp.int32)
    earlier = positions[None, :] < positions[:, None]
    same_owner = owner_list[:, None] == owner_list[None, :]
    rank_of = jnp.sum(same_owner & earlier, axis=1)
    owner_ids = jnp.arange(owner_count, dtype=jnp.int32)
    slot_ids = jnp.arange(slot_count, dtype=jnp.int32)
    return (owner_list[None, None, :] == owner_ids[:, None, None]) & (
        rank_of[None, None, :] == slot_ids[None, :, None]
    )


def attend_rows(query_rows, key_win, value_win, first_key, row_ids, row_starts):
    query_count = query_rows.shape[0]
    key_span = key_win.shape[0]
    kv_heads = key_win.shape[1] // HEAD_WIDTH
    query_group_width = query_rows.shape[1] // (kv_heads * HEAD_WIDTH)
    heads_for_query = query_rows.reshape(query_count, kv_heads, query_group_width, HEAD_WIDTH)
    heads_for_key = key_win.reshape(key_span, kv_heads, HEAD_WIDTH)
    value_heads = value_win.reshape(key_span, kv_heads, HEAD_WIDTH)
    scores = jnp.einsum(
        "tkgd,jkd->tkgj", heads_for_query, heads_for_key, preferred_element_type=jnp.float32
    ) / math.sqrt(HEAD_WIDTH)
    key_ids = first_key + jnp.arange(key_span, dtype=jnp.int32)
    allowed = (key_ids[None, :] >= row_starts[:, None]) & (key_ids[None, :] <= row_ids[:, None])
    scores = jnp.where(allowed[:, None, None, :], scores, -1e30)
    row_max = jnp.max(scores, axis=-1, keepdims=True)
    exp_terms = jnp.exp(scores - row_max)
    denom_sum = jnp.sum(exp_terms, axis=-1)
    weights = exp_terms.astype(jnp.bfloat16)
    attended = (
        jnp.einsum("tkgj,jkd->tkgd", weights, value_heads, preferred_element_type=jnp.float32)
        / denom_sum[..., None]
    )
    return attended.reshape(query_count, -1).astype(jnp.bfloat16)


def local(queries, keys, values, doc_start, owners):
    section_index = lax.axis_index("pipe")
    my_ctx = lax.axis_index("ctx")
    ctx_count = lax.axis_size("ctx")
    micro_count = queries.shape[1]
    rows_dev = queries.shape[2]
    width_q = queries.shape[3]
    width_kv = keys.shape[3]
    tract_rows = rows_dev // TRACTS_DEV
    slot_count = TRACTS_DEV // ctx_count + 1
    local_ids = jnp.arange(tract_rows, dtype=jnp.int32)
    carried = jnp.zeros((ctx_count, slot_count, tract_rows, width_q), jnp.bfloat16)
    tick_outputs = []
    for clock_tick in range(micro_count + 1):
        mb_index = clock_tick - section_index
        mb_pick = jnp.clip(mb_index, 0, micro_count - 1)
        own_queries = lax.dynamic_index_in_dim(queries[0], mb_pick, 0, keepdims=False)
        key_rows = lax.dynamic_index_in_dim(keys[0], mb_pick, 0, keepdims=False)
        value_rows = lax.dynamic_index_in_dim(values[0], mb_pick, 0, keepdims=False)
        own_list = lax.dynamic_index_in_dim(owners, mb_pick, 0, keepdims=False)
        send_map = rank_table(own_list, ctx_count, slot_count).astype(jnp.bfloat16)
        tract_block = own_queries.reshape(TRACTS_DEV, tract_rows, width_q)
        outgoing = jnp.einsum(
            "osk,ktf->ostf", send_map, tract_block, preferred_element_type=jnp.float32
        ).astype(jnp.bfloat16)
        arrived = lax.all_to_all(outgoing, "ctx", split_axis=0, concat_axis=0, tiled=True)
        all_keys, all_values, all_owners, all_starts = (
            lax.all_gather(key_rows, "ctx", axis=0, tiled=True),
            lax.all_gather(value_rows, "ctx", axis=0, tiled=True),
            lax.all_gather(owners, "ctx", axis=1, tiled=True),
            lax.all_gather(doc_start, "ctx", axis=1, tiled=True),
        )
        section_in = (arrived.astype(jnp.float32) + carried.astype(jnp.float32)).astype(
            jnp.bfloat16
        )
        lists = lax.dynamic_index_in_dim(all_owners, mb_pick, 0, keepdims=False).reshape(
            ctx_count, TRACTS_DEV
        )
        starts_all = lax.dynamic_index_in_dim(all_starts, mb_pick, 0, keepdims=False)

        def table_of(block_list):
            return rank_table(block_list, ctx_count, slot_count)

        tables = jax.vmap(table_of)(lists)
        mine = lax.dynamic_index_in_dim(tables, my_ctx, 1, keepdims=False)
        present = jnp.any(mine, axis=2)
        tract_pos = jnp.sum(
            mine.astype(jnp.int32) * jnp.arange(TRACTS_DEV, dtype=jnp.int32), axis=2
        )
        first_rows = (
            jnp.arange(ctx_count, dtype=jnp.int32)[:, None] * rows_dev + tract_pos * tract_rows
        )
        row_grid = first_rows[..., None] + local_ids
        start_grid = starts_all[row_grid]
        padded_keys = jnp.concatenate(
            [jnp.zeros((DOCMAX, width_kv), jnp.bfloat16), all_keys], axis=0
        )
        padded_values = jnp.concatenate(
            [jnp.zeros((DOCMAX, width_kv), jnp.bfloat16), all_values], axis=0
        )
        source_answers = []
        for source_id in range(ctx_count):
            key_win = padded_keys[source_id * rows_dev : source_id * rows_dev + rows_dev + DOCMAX]
            value_win = padded_values[
                source_id * rows_dev : source_id * rows_dev + rows_dev + DOCMAX
            ]
            slot_queries = section_in[source_id].reshape(slot_count * tract_rows, width_q)
            slot_ids = row_grid[source_id].reshape(-1)
            slot_starts = start_grid[source_id].reshape(-1)
            answer = attend_rows(
                slot_queries,
                key_win,
                value_win,
                source_id * rows_dev - DOCMAX,
                slot_ids,
                slot_starts,
            )
            source_answers.append(answer.reshape(slot_count, tract_rows, width_q))
        answers = jnp.stack(source_answers)
        owner_rows = jnp.where(present[:, :, None, None], answers, jnp.zeros_like(answers))
        if clock_tick < micro_count:
            carried = shifted(owner_rows, "pipe", 1)
        tick_outputs.append(owner_rows)
    first_section = section_index == 0
    result = jnp.stack(
        [
            jnp.where(first_section, tick_outputs[micro_id], tick_outputs[micro_id + 1])
            for micro_id in range(micro_count)
        ]
    )
    return result[None, :, None]


def solution(mesh):
    return jax.shard_map(
        local,
        mesh=mesh,
        in_specs=(
            P("pipe", None, "ctx", "tp"),
            P("pipe", None, "ctx", "tp"),
            P("pipe", None, "ctx", "tp"),
            P(None, "ctx"),
            P(None, "ctx"),
        ),
        out_specs=P("pipe", None, "ctx", None, None, None, "tp"),
        check_vma=False,
    )
```

profile of v0, /device:TPU:6, one launch (start us, length us, event | category | flops | bytes accessed | tf_op | source)
XLA Modules:
  0.0 336.8 jit_solution(15088686143844010737)
XLA Ops:
  6.5 1.9 constant_dynamic-slice_fusion.16
  8.6 1.8 constant_dynamic-slice_fusion.4
  12.7 1.7 constant_dynamic-slice_fusion
  14.4 0.9 convolution_convert_fusion.2
  15.3 2.0 copy.204
  17.3 6.9 %all-to-all-start = ((bf16[8,3,32,1024]{3,2,1,0:T(8,128)(2,1)}), bf16[8,3,32,1024]{3,2,1,0:T(8,128)(2,1)S(1)}, u32[]{:S(2)}, u32[]{:S(2)}) async-start(bf16[8,3,32,1024]{3,2,1,0:T(8,128)(2,1)} %copy.204), calls=%async_computation | async-start | bytes 3145728 | tf_op jit(solution)/shard_map/all_to_all | solution.py:81
  24.8 36.3 %all-gather.6 = s32[8,16,2]{1,2,0:T(2,128)S(1)} all-gather(s32[1,16,2]{1,2,0:T(2,128)S(1)} %bitcast.1570), channel_id=1, replica_groups=mesh['pipe'=2,'ctx'=8,'tp'=8] {'ctx'}, dimensions={0}, use_global_device_ids=true | all-gather | bytes 1152 | tf_op jit(solution)/shard_map/all_gather | solution.py:85
  63.8 28.1 %all_gather.30 = s32[2,4096]{1,0:T(2,128)S(1)} all-gather(s32[2,512]{1,0:T(2,128)S(1)} %copy-done.96), channel_id=1, replica_groups=mesh['pipe'=2,'ctx'=8,'tp'=8] {'ctx'}, dimensions={1}, use_global_device_ids=true | all-gather | bytes 36864 | tf_op jit(solution)/shard_map/all_gather | solution.py:86
  91.9 4.5 %gather_fusion.1 = s32[768]{0:T(1024)S(1)} fusion(s32[4096]{0:T(1024)S(1)} %bitcast.1515, s32[1024]{0:T(1024)S(1)} %pad_clamp_fusion.1), kind=kCustom, calls=%fused_computation.1 | custom fusion | bytes 9216 | tf_op jit(solution)/shard_map/gather | solution.py:109
  96.5 4.5 %gather_fusion = s32[768]{0:T(1024)S(1)} fusion(s32[4096]{0:T(1024)S(1)} %bitcast.1514, s32[1024]{0:T(1024)S(1)} %pad_clamp_fusion.2), kind=kCustom, calls=%fused_computation | custom fusion | bytes 9216 | tf_op jit(solution)/shard_map/gather | solution.py:109
  101.4 4.9 %gather_fusion.2 = s32[768]{0:T(1024)S(1)} fusion(s32[4096]{0:T(1024)S(1)} %bitcast.1513, s32[1024]{0:T(1024)S(1)} %pad_clamp_fusion), kind=kCustom, calls=%fused_computation.2 | custom fusion | bytes 9216 | tf_op jit(solution)/shard_map/gather | solution.py:109
  108.2 0.9 compare_and_fusion.6
  109.1 0.9 compare_and_fusion.7
  110.0 0.9 compare_and_fusion.5
  113.4 0.9 compare_and_fusion.4
  114.3 0.9 compare_and_fusion.3
  115.2 0.9 compare_and_fusion.2
  116.1 0.9 compare_and_fusion.1
  117.0 0.9 compare_and_fusion
  123.1 1.5 fusion.48
  124.6 1.3 fusion
  125.8 1.8 fusion.429
  127.9 1.6 fusion.49
  143.0 1.4 fusion.408
  147.5 1.0 copy.220
  149.4 1.0 constant_dynamic-update-slice_fusion.11
  150.5 0.9 constant_dynamic-update-slice_fusion.10
  151.4 0.9 constant_dynamic-update-slice_fusion.9
  152.4 1.3 broadcast_select_fusion.1
  153.7 1.3 collective-permute-start
  155.1 0.9 convolution_convert_fusion.1
  155.9 2.0 copy.225
  158.0 3.7 %all-to-all-start.1 = ((bf16[8,3,32,1024]{3,2,1,0:T(8,128)(2,1)}), bf16[8,3,32,1024]{3,2,1,0:T(8,128)(2,1)S(1)}, u32[]{:S(2)}, u32[]{:S(2)}) async-start(bf16[8,3,32,1024]{3,2,1,0:T(8,128)(2,1)} %copy.225), calls=%async_computation.1 | async-start | bytes 3145728 | tf_op jit(solution)/shard_map/all_to_all | solution.py:81
  164.0 2.0 copy.255
  169.2 9.8 %all-to-all-done.1 = bf16[8,3,32,1024]{3,2,1,0:T(8,128)(2,1)S(1)} async-done(((bf16[8,3,32,1024]{3,2,1,0:T(8,128)(2,1)}), bf16[8,3,32,1024]{3,2,1,0:T(8,128)(2,1)S(1)}, u32[]{:S(2)}, u32[]{:S(2)}) %all-to-all-start.1) | async-done | bytes 1572896 | tf_op jit(solution)/shard_map/all_to_all | solution.py:81
  179.0 5.9 %all-to-all-start.2 = ((bf16[8,3,32,1024]{3,2,1,0:T(8,128)(2,1)}), bf16[8,3,32,1024]{3,2,1,0:T(8,128)(2,1)}, u32[]{:S(2)}, u32[]{:S(2)}) async-start(bf16[8,3,32,1024]{3,2,1,0:T(8,128)(2,1)} %copy.255), calls=%async_computation.2 | async-start | bytes 3145728 | tf_op jit(solution)/shard_map/all_to_all | solution.py:81
  184.9 15.6 %collective-permute-done = bf16[8,3,32,1024]{3,2,1,0:T(8,128)(2,1)} collective-permute-done((bf16[8,3,32,1024]{3,2,1,0:T(8,128)(2,1)}, bf16[8,3,32,1024]{3,2,1,0:T(8,128)(2,1)}, u32[]{:S(2)}, u32[]{:S(2)}) %collective-permute-start) | collective-permute-done | bytes 1572896 | tf_op jit(solution)/shard_map/ppermute | solution.py:15
  200.5 2.1 add_convert_fusion.1
  202.7 1.1 fusion.571
  203.9 1.6 fusion.57
  206.0 1.3 fusion.18
  207.3 1.7 fusion.402
  209.2 1.0 copy.293
  214.6 1.7 fusion.399
  217.9 1.7 fusion.396
  221.8 1.7 fusion.393
  226.0 1.7 fusion.390
  229.9 1.7 fusion.387
  233.9 1.7 fusion.384
  236.7 1.3 broadcast_select_fusion
  238.1 1.4 collective-permute-start.1
  250.6 45.0 %collective-permute-done.1 = bf16[8,3,32,1024]{3,2,1,0:T(8,128)(2,1)} collective-permute-done((bf16[8,3,32,1024]{3,2,1,0:T(8,128)(2,1)}, bf16[8,3,32,1024]{3,2,1,0:T(8,128)(2,1)}, u32[]{:S(2)}, u32[]{:S(2)}) %collective-permute-start.1) | collective-permute-done | bytes 1572896 | tf_op jit(solution)/shard_map/ppermute | solution.py:15
  295.6 2.6 add_convert_fusion
  298.2 1.1 fusion.570
  299.4 1.6 fusion.71
  301.6 1.3 fusion.46
  302.8 1.7 fusion.360
  304.7 1.0 copy.307
  313.3 0.9 fusion.38
  314.2 1.7 fusion.372
  317.5 1.7 fusion.375
  320.8 1.7 fusion.378
  325.5 2.3 select_select_fusion.1
  327.8 1.9 maximum_bitcast_fusion
  (491 shorter events, 79.7 us)
Async XLA Ops:
  6.5 6.1 %copy-start.3 = (bf16[1,2,512,1024]{3,2,1,0:T(8,128)(2,1)S(1)}, bf16[1,2,512,1024]{3,2,1,0:T(8,128)(2,1)}, u32[]{:S(2)}) copy-start(bf16[1,2,512,1024]{3,2,1,0:T(8,128)(2,1)} %param.5) | copy-start | bytes 6291460
  6.5 116.6 %all-gather.16.cloned.1.call-start = ((), (), s32[]{:S(2)}) async-start(), calls=%async_computation.4 | async-start | bytes 1179648 | tf_op jit(solution)/shard_map/all_gather | solution.py:83
  8.5 117.3 %all-gather.14.cloned.1.call-start = ((), (), s32[]{:S(2)}) async-start(), calls=%async_computation.3 | async-start | bytes 1179648 | tf_op jit(solution)/shard_map/all_gather | solution.py:84
  10.4 193.5 %all-gather.20.cloned.1.call-start = ((), (), s32[]{:S(2)}) async-start(), calls=%async_computation.6 | async-start | bytes 1179648 | tf_op jit(solution)/shard_map/all_gather | solution.py:83
  11.1 196.2 %all-gather.18.cloned.1.call-start = ((), (), s32[]{:S(2)}) async-start(), calls=%async_computation.5 | async-start | bytes 1179648 | tf_op jit(solution)/shard_map/all_gather | solution.py:84
  17.3 7.5 %copy-start.89 = (s32[2,16]{1,0:T(2,128)S(1)}, s32[2,16]{1,0:T(2,128)}, u32[]{:S(2)}) copy-start(s32[2,16]{1,0:T(2,128)} %param.9) | copy-start | bytes 388
  17.3 46.5 %copy-start.96 = (s32[2,512]{1,0:T(2,128)S(1)}, s32[2,512]{1,0:T(2,128)}, u32[]{:S(2)}) copy-start(s32[2,512]{1,0:T(2,128)} %param.8) | copy-start | bytes 12292
  17.3 100.6 %all-to-all-start = ((bf16[8,3,32,1024]{3,2,1,0:T(8,128)(2,1)}), bf16[8,3,32,1024]{3,2,1,0:T(8,128)(2,1)S(1)}, u32[]{:S(2)}, u32[]{:S(2)}) async-start(bf16[8,3,32,1024]{3,2,1,0:T(8,128)(2,1)} %copy.204), calls=%async_computation | async-start | bytes 3145728 | tf_op jit(solution)/shard_map/all_to_all | solution.py:81
  24.2 275.2 %all-gather.24.cloned.1.call-start = ((), (), s32[]{:S(2)}) async-start(), calls=%async_computation.8 | async-start | bytes 1179648 | tf_op jit(solution)/shard_map/all_gather | solution.py:83
  118.1 5.0 %copy-start.77 = (pred[96,768]{1,0:T(8,128)(4,1)S(1)}, pred[96,768]{1,0:T(8,128)(4,1)}, u32[]{:S(2)}) copy-start(pred[96,768]{1,0:T(8,128)(4,1)} %get-tuple-element.103) | copy-start | bytes 221188
  127.8 2.4 copy-start.18
  127.9 2.3 copy-start.55
  144.9 5.6 %copy-start.6 = (bf16[96,1,8,128]{3,2,0,1:T(8,128)(2,1)}, bf16[96,1,8,128]{3,2,0,1:T(8,128)(2,1)S(1)}, u32[]{:S(2)}) copy-start(bf16[96,1,8,128]{3,2,0,1:T(8,128)(2,1)S(1)} %copy.212) | copy-start | bytes 589828
  145.0 7.3 %copy-start.8 = (bf16[96,1,8,128]{3,2,0,1:T(8,128)(2,1)}, bf16[96,1,8,128]{3,2,0,1:T(8,128)(2,1)S(1)}, u32[]{:S(2)}) copy-start(bf16[96,1,8,128]{3,2,0,1:T(8,128)(2,1)S(1)} %copy.214) | copy-start | bytes 589828
  145.9 7.8 %copy-start.10 = (bf16[96,1,8,128]{3,2,0,1:T(8,128)(2,1)}, bf16[96,1,8,128]{3,2,0,1:T(8,128)(2,1)S(1)}, u32[]{:S(2)}) copy-start(bf16[96,1,8,128]{3,2,0,1:T(8,128)(2,1)S(1)} %copy.216) | copy-start | bytes 589828
  145.9 6.5 %copy-start.90 = (pred[8,3]{1,0:T(8,128)(4,1)S(1)}, pred[8,3]{1,0:T(8,128)(4,1)}, u32[]{:S(2)}) copy-start(pred[8,3]{1,0:T(8,128)(4,1)} %copy.200) | copy-start | bytes 76
  146.8 7.0 %copy-start.12 = (bf16[96,1,8,128]{3,2,0,1:T(8,128)(2,1)}, bf16[96,1,8,128]{3,2,0,1:T(8,128)(2,1)S(1)}, u32[]{:S(2)}) copy-start(bf16[96,1,8,128]{3,2,0,1:T(8,128)(2,1)S(1)} %copy.218) | copy-start | bytes 589828
  148.6 5.2 %copy-start.14 = (bf16[96,1,8,128]{3,2,0,1:T(8,128)(2,1)}, bf16[96,1,8,128]{3,2,0,1:T(8,128)(2,1)S(1)}, u32[]{:S(2)}) copy-start(bf16[96,1,8,128]{3,2,0,1:T(8,128)(2,1)S(1)} %copy.220) | copy-start | bytes 589828
  149.3 3.0 copy-start.49
  149.4 5.6 %copy-start.5 = (bf16[1,1,512,1024]{3,2,1,0:T(8,128)(2,1)S(1)}, bf16[1,1,512,1024]{3,2,1,0:T(8,128)(2,1)}, u32[]{:S(2)}) copy-start(bf16[1,1,512,1024]{3,2,1,0:T(8,128)(2,1)} %get-tuple-element.13) | copy-start | bytes 3145732
  149.4 5.6 %copy-start.95 = (pred[8,16]{1,0:T(8,128)(4,1)S(1)}, pred[8,16]{1,0:T(8,128)(4,1)}, u32[]{:S(2)}) copy-start(pred[8,16]{1,0:T(8,128)(4,1)} %get-tuple-element.182) | copy-start | bytes 388
  149.4 5.6 %copy-start.99 = (pred[3,16]{1,0:T(4,128)(4,1)S(1)}, pred[3,16]{1,0:T(4,128)(4,1)}, u32[]{:S(2)}) copy-start(pred[3,16]{1,0:T(4,128)(4,1)} %iota_compare_fusion.11) | copy-start | bytes 148
  153.7 46.8 %collective-permute-start = (bf16[8,3,32,1024]{3,2,1,0:T(8,128)(2,1)}, bf16[8,3,32,1024]{3,2,1,0:T(8,128)(2,1)}, u32[]{:S(2)}, u32[]{:S(2)}) collective-permute-start(bf16[8,3,32,1024]{3,2,1,0:T(8,128)(2,1)} %broadcast_select_fusion.1), channel_id=1, source_target_pairs={{0,64},{1,65},{2,66},{3,67},{4,68},{5,69},{6,70},{7,71},{8,72},{9,... | collective-permute-start | bytes 4718600 | tf_op jit(solution)/shard_map/ppermute | solution.py:15
  157.9 4.3 %copy-start.81 = (pred[8,3,16]{2,0,1:T(8,128)(4,1)S(1)}, pred[8,3,16]{2,0,1:T(8,128)(4,1)}, u32[]{:S(2)}) copy-start(pred[8,3,16]{2,0,1:T(8,128)(4,1)} %copy-done.80) | copy-start | bytes 1156
  158.0 4.3 %copy-start.88 = (pred[8,1,16]{2,0,1:T(8,128)(4,1)S(1)}, pred[8,1,16]{2,0,1:T(8,128)(4,1)}, u32[]{:S(2)}) copy-start(pred[8,1,16]{2,0,1:T(8,128)(4,1)} %copy-done.87) | copy-start | bytes 388
  158.0 5.1 %copy-start.98 = (s32[16]{0:T(128)S(1)}, s32[16]{0:T(128)}, u32[]{:S(2)}) copy-start(s32[16]{0:T(128)} %get-tuple-element.179) | copy-start | bytes 196
  158.0 5.1 %copy-start.4 = (bf16[1,1,512,1024]{3,2,1,0:T(8,128)(2,1)S(1)}, bf16[1,1,512,1024]{3,2,1,0:T(8,128)(2,1)}, u32[]{:S(2)}) copy-start(bf16[1,1,512,1024]{3,2,1,0:T(8,128)(2,1)} %get-tuple-element.11) | copy-start | bytes 3145732
  158.0 5.1 %copy-start.94 = (pred[8,16]{1,0:T(8,128)(4,1)S(1)}, pred[8,16]{1,0:T(8,128)(4,1)}, u32[]{:S(2)}) copy-start(pred[8,16]{1,0:T(8,128)(4,1)} %get-tuple-element.181) | copy-start | bytes 388
  158.0 21.0 %all-to-all-start.1 = ((bf16[8,3,32,1024]{3,2,1,0:T(8,128)(2,1)}), bf16[8,3,32,1024]{3,2,1,0:T(8,128)(2,1)S(1)}, u32[]{:S(2)}, u32[]{:S(2)}) async-start(bf16[8,3,32,1024]{3,2,1,0:T(8,128)(2,1)} %copy.225), calls=%async_computation.1 | async-start | bytes 3145728 | tf_op jit(solution)/shard_map/all_to_all | solution.py:81
  161.7 141.2 %all-gather.22.cloned.1.call-start = ((), (), s32[]{:S(2)}) async-start(), calls=%async_computation.7 | async-start | bytes 1179648 | tf_op jit(solution)/shard_map/all_gather | solution.py:84
  163.1 2.9 copy-start.79
  163.1 2.9 copy-start.86
  164.0 3.7 %copy-start.19 = (bf16[96,1,8,128]{3,2,0,1:T(8,128)(2,1)S(1)}, bf16[96,1,8,128]{3,2,0,1:T(8,128)(2,1)}, u32[]{:S(2)}) copy-start(bf16[96,1,8,128]{3,2,0,1:T(8,128)(2,1)} %copy-done.18) | copy-start | bytes 589828
  179.0 71.6 %all-to-all-start.2 = ((bf16[8,3,32,1024]{3,2,1,0:T(8,128)(2,1)}), bf16[8,3,32,1024]{3,2,1,0:T(8,128)(2,1)}, u32[]{:S(2)}, u32[]{:S(2)}) async-start(bf16[8,3,32,1024]{3,2,1,0:T(8,128)(2,1)} %copy.255), calls=%async_computation.2 | async-start | bytes 3145728 | tf_op jit(solution)/shard_map/all_to_all | solution.py:81
  207.3 2.9 copy-start.1
  207.3 2.9 copy-start.76
  209.1 2.3 copy-start.16
  217.9 2.6 copy-start.39
  217.9 2.6 copy-start.68
  219.7 2.1 copy-start.24
  221.8 2.6 copy-start.37
  221.8 2.6 copy-start.67
  223.6 2.3 copy-start.26
  226.0 2.6 copy-start.35
  226.0 2.6 copy-start.66
  229.9 2.6 copy-start.33
  229.9 2.6 copy-start.65
  231.7 2.1 copy-start.30
  235.9 3.6 %copy-start.44 = (bf16[1,1,3,32,1024]{4,3,2,1,0:T(8,128)(2,1)S(1)}, bf16[1,1,3,32,1024]{4,3,2,1,0:T(8,128)(2,1)}, u32[]{:S(2)}) copy-start(bf16[1,1,3,32,1024]{4,3,2,1,0:T(8,128)(2,1)} %stack.68) | copy-start | bytes 589828
  236.5 3.7 %copy-start.15 = (bf16[96,1,8,128]{3,2,0,1:T(8,128)(2,1)S(1)}, bf16[96,1,8,128]{3,2,0,1:T(8,128)(2,1)}, u32[]{:S(2)}) copy-start(bf16[96,1,8,128]{3,2,0,1:T(8,128)(2,1)} %copy-done.14) | copy-start | bytes 589828
  236.6 3.7 %copy-start.13 = (bf16[96,1,8,128]{3,2,0,1:T(8,128)(2,1)S(1)}, bf16[96,1,8,128]{3,2,0,1:T(8,128)(2,1)}, u32[]{:S(2)}) copy-start(bf16[96,1,8,128]{3,2,0,1:T(8,128)(2,1)} %copy-done.12) | copy-start | bytes 589828
  236.7 3.8 %copy-start.11 = (bf16[96,1,8,128]{3,2,0,1:T(8,128)(2,1)S(1)}, bf16[96,1,8,128]{3,2,0,1:T(8,128)(2,1)}, u32[]{:S(2)}) copy-start(bf16[96,1,8,128]{3,2,0,1:T(8,128)(2,1)} %copy-done.10) | copy-start | bytes 589828
  236.7 3.8 %copy-start.9 = (bf16[96,1,8,128]{3,2,0,1:T(8,128)(2,1)S(1)}, bf16[96,1,8,128]{3,2,0,1:T(8,128)(2,1)}, u32[]{:S(2)}) copy-start(bf16[96,1,8,128]{3,2,0,1:T(8,128)(2,1)} %copy-done.8) | copy-start | bytes 589828
  236.7 3.9 %copy-start.7 = (bf16[96,1,8,128]{3,2,0,1:T(8,128)(2,1)S(1)}, bf16[96,1,8,128]{3,2,0,1:T(8,128)(2,1)}, u32[]{:S(2)}) copy-start(bf16[96,1,8,128]{3,2,0,1:T(8,128)(2,1)} %copy-done.6) | copy-start | bytes 589828
  238.1 6.2 %copy-start.31 = (bf16[96,1,8,128]{3,2,0,1:T(8,128)(2,1)S(1)}, bf16[96,1,8,128]{3,2,0,1:T(8,128)(2,1)}, u32[]{:S(2)}) copy-start(bf16[96,1,8,128]{3,2,0,1:T(8,128)(2,1)} %copy-done.30) | copy-start | bytes 589828
  238.1 57.5 %collective-permute-start.1 = (bf16[8,3,32,1024]{3,2,1,0:T(8,128)(2,1)}, bf16[8,3,32,1024]{3,2,1,0:T(8,128)(2,1)}, u32[]{:S(2)}, u32[]{:S(2)}) collective-permute-start(bf16[8,3,32,1024]{3,2,1,0:T(8,128)(2,1)} %broadcast_select_fusion), channel_id=1, source_target_pairs={{0,64},{1,65},{2,66},{3,67},{4,68},{5,69},{6,70},{7,71},{8,72},{9,... | collective-permute-start | bytes 4718600 | tf_op jit(solution)/shard_map/ppermute | solution.py:15
  240.2 4.2 %copy-start.29 = (bf16[96,1,8,128]{3,2,0,1:T(8,128)(2,1)S(1)}, bf16[96,1,8,128]{3,2,0,1:T(8,128)(2,1)}, u32[]{:S(2)}) copy-start(bf16[96,1,8,128]{3,2,0,1:T(8,128)(2,1)} %copy-done.28) | copy-start | bytes 589828
  240.3 4.2 %copy-start.27 = (bf16[96,1,8,128]{3,2,0,1:T(8,128)(2,1)S(1)}, bf16[96,1,8,128]{3,2,0,1:T(8,128)(2,1)}, u32[]{:S(2)}) copy-start(bf16[96,1,8,128]{3,2,0,1:T(8,128)(2,1)} %copy-done.26) | copy-start | bytes 589828
  240.4 4.2 %copy-start.25 = (bf16[96,1,8,128]{3,2,0,1:T(8,128)(2,1)S(1)}, bf16[96,1,8,128]{3,2,0,1:T(8,128)(2,1)}, u32[]{:S(2)}) copy-start(bf16[96,1,8,128]{3,2,0,1:T(8,128)(2,1)} %copy-done.24) | copy-start | bytes 589828
  240.5 4.2 %copy-start.23 = (bf16[96,1,8,128]{3,2,0,1:T(8,128)(2,1)S(1)}, bf16[96,1,8,128]{3,2,0,1:T(8,128)(2,1)}, u32[]{:S(2)}) copy-start(bf16[96,1,8,128]{3,2,0,1:T(8,128)(2,1)} %copy-done.22) | copy-start | bytes 589828
  240.7 4.2 %copy-start.17 = (bf16[96,1,8,128]{3,2,0,1:T(8,128)(2,1)S(1)}, bf16[96,1,8,128]{3,2,0,1:T(8,128)(2,1)}, u32[]{:S(2)}) copy-start(bf16[96,1,8,128]{3,2,0,1:T(8,128)(2,1)} %copy-done.16) | copy-start | bytes 589828
  240.8 4.2 %copy-start.21 = (bf16[96,1,8,128]{3,2,0,1:T(8,128)(2,1)S(1)}, bf16[96,1,8,128]{3,2,0,1:T(8,128)(2,1)}, u32[]{:S(2)}) copy-start(bf16[96,1,8,128]{3,2,0,1:T(8,128)(2,1)} %copy-done.20) | copy-start | bytes 589828
  302.8 2.9 copy-start
  302.8 2.9 copy-start.61
  (51 other events, 66.7 us)
Sparse Core Ops, SparseCore 0:
  9.0 51.1 all-gather.15
  61.8 38.1 all-gather.13
  101.7 38.0 all-gather.19
  141.3 48.4 all-gather.17
  191.3 39.7 all-gather.23
  232.5 43.8 all-gather.21
where the time goes:
time: 342 us; the launch traced here: 337 us
  waiting for transfers between devices  72.9 us (21%)
  local copies, waits for them, and re-layouts  70.8 us (21%)
  blocking collectives  64.4 us (19%)
  matrix products  52.2 us (15%)
  other arithmetic  40.9 us (12%)
  starting transfers between devices  19.3 us (6%)
  between operations  16.2 us (5%)
    ppermute x2, waiting for transfers between devices, shifted(): return lax.ppermute(block, axis, route)  60.7 us
    all_gather x1, blocking collectives, local(): lax.all_gather(owners, 'ctx', axis=1, tiled=True)  36.3 us
    dot_general x24, matrix products, attend_rows(): jnp.einsum('tkgj,jkd->tkgd', weights, value_heads, preferred_element_type...  30.3 us
    all_gather x1, blocking collectives, local(): lax.all_gather(doc_start, 'ctx', axis=1, tiled=True)  28.1 us
    unnamed x269, local copies, waits for them, and re-layouts  23.5 us
    dot_general x24, matrix products, attend_rows(): jnp.einsum('tkgd,jkd->tkgj', heads_for_query, heads_for_key, preferred_el...  19.3 us
    reduce_sum x24, other arithmetic, attend_rows(): denom_sum = jnp.sum(exp_terms, axis=-1)  18 us
    all_to_all x3, starting transfers between devices, local(): lax.all_to_all(outgoing, 'ctx', split_axis=0, concat_axis=0, tiled=True)  16.4 us
  transfers between devices with their start and end apart: 11, of which 3 were waited for; matrix products, arithmetic and copies ran while one was open for 39% of the time, Pallas kernels for 0%

commit v1 on v0

--- a/solution.py
+++ b/solution.py
@@ -7,6 +7,13 @@
 HEAD_WIDTH = 128
 TRACTS_DEV = 16
 DOCMAX = 256
+
+
+def begin_edges(t0):
+    opened = lax.axis_size("ctx")
+    reply = jnp.stack(opened * [t0], axis=0)
+    z = lax.all_to_all(reply, "ctx", 0, 0)
+    return jnp.concatenate(z, axis=1)
 
 
 def shifted(block, axis, distance):
@@ -83,7 +90,7 @@
             lax.all_gather(key_rows, "ctx", axis=0, tiled=True),
             lax.all_gather(value_rows, "ctx", axis=0, tiled=True),
             lax.all_gather(owners, "ctx", axis=1, tiled=True),
-            lax.all_gather(doc_start, "ctx", axis=1, tiled=True),
+            begin_edges(doc_start),
         )
         section_in = (arrived.astype(jnp.float32) + carried.astype(jnp.float32)).astype(
             jnp.bfloat16

time: 342 us -> 320 us (0.936)
  blocking collectives: 64.4 us -> 17.8 us
  waiting for transfers between devices: 72.9 us -> 90.2 us
  starting transfers between devices: 19.3 us -> 25.6 us
    all_gather x1 -> x0, blocking collectives: 28.1 us -> none  [local(): lax.all_gather(doc_start, 'ctx', axis=1, tiled=True)]
    all_gather x3, waiting for transfers between devices: 0.01 us -> 19.1 us  [local(): lax.all_gather(value_rows, 'ctx', axis=0, tiled=True)]
    all_gather x1, blocking collectives: 36.3 us -> 17.8 us  [local(): lax.all_gather(owners, 'ctx', axis=1, tiled=True)]
    all_to_all x0 -> x1, starting transfers between devices: none -> 6.77 us  [begin_edges(): z = lax.all_to_all(reply, 'ctx', 0, 0)]
    unnamed x269 -> x267, local copies, waits for them, and re-layouts: 23.5 us -> 23.5 us
  transfers between devices with their start and end apart: 11 -> 12, of which waited for: 3 -> 5; matrix products, arithmetic and copies ran while one was open for 39% -> 42% of each run, Pallas kernels for 0% -> 0%
where the time goes in v1:
time: 320 us; the launch traced here: 314 us
  waiting for transfers between devices  90.2 us (28%)
  local copies, waits for them, and re-layouts  71.4 us (22%)
  matrix products  52.2 us (16%)
  other arithmetic  40.9 us (13%)
  starting transfers between devices  25.6 us (8%)
  blocking collectives  17.8 us (6%)
  between operations  16.2 us (5%)
    ppermute x2, waiting for transfers between devices, shifted(): return lax.ppermute(block, axis, route)  59.3 us
    dot_general x24, matrix products, attend_rows(): jnp.einsum('tkgj,jkd->tkgd', weights, value_heads, preferred_element_type...  30.2 us
    unnamed x267, local copies, waits for them, and re-layouts  23.5 us
    dot_general x24, matrix products, attend_rows(): jnp.einsum('tkgd,jkd->tkgj', heads_for_query, heads_for_key, preferred_el...  19.3 us
    all_gather x3, waiting for transfers between devices, local(): lax.all_gather(value_rows, 'ctx', axis=0, tiled=True)  19.1 us
    reduce_sum x24, other arithmetic, attend_rows(): denom_sum = jnp.sum(exp_terms, axis=-1)  18 us
    all_gather x1, blocking collectives, local(): lax.all_gather(owners, 'ctx', axis=1, tiled=True)  17.8 us
    all_to_all x3, starting transfers between devices, local(): lax.all_to_all(outgoing, 'ctx', split_axis=0, concat_axis=0, tiled=True)  16 us
  transfers between devices with their start and end apart: 12, of which 5 were waited for; matrix products, arithmetic and copies ran while one was open for 42% of the time, Pallas kernels for 0%

profile of v1, /device:TPU:6, one launch (start us, length us, event | category | flops | bytes accessed | tf_op | source)
XLA Modules:
  0.0 314.2 jit_solution(14526371864968663006)
XLA Ops:
  6.5 1.9 constant_dynamic-slice_fusion.16
  8.6 1.8 constant_dynamic-slice_fusion.4
  11.7 1.3 stack.95
  13.0 6.8 %all-to-all-start = ((s32[8,2,512]{2,1,0:T(2,128)}), s32[8,2,512]{2,1,0:T(2,128)S(1)}, u32[]{:S(2)}, u32[]{:S(2)}) async-start(s32[8,2,512]{2,1,0:T(2,128)} %stack.95), calls=%async_computation | async-start | bytes 65536 | tf_op jit(solution)/shard_map/all_to_all | solution.py:15
  20.4 17.8 %all-gather.6 = s32[8,16,2]{1,2,0:T(2,128)S(1)} all-gather(s32[1,16,2]{1,2,0:T(2,128)S(1)} %bitcast.1574), channel_id=1, replica_groups=mesh['pipe'=2,'ctx'=8,'tp'=8] {'ctx'}, dimensions={0}, use_global_device_ids=true | all-gather | bytes 1152 | tf_op jit(solution)/shard_map/all_gather | solution.py:92
  42.5 1.7 constant_dynamic-slice_fusion
  45.9 2.0 copy.204
  50.3 5.0 %all-to-all-start.1 = ((bf16[8,3,32,1024]{3,2,1,0:T(8,128)(2,1)}), bf16[8,3,32,1024]{3,2,1,0:T(8,128)(2,1)S(1)}, u32[]{:S(2)}, u32[]{:S(2)}) async-start(bf16[8,3,32,1024]{3,2,1,0:T(8,128)(2,1)} %copy.204), calls=%async_computation.1 | async-start | bytes 3145728 | tf_op jit(solution)/shard_map/all_to_all | solution.py:88
  55.3 4.5 %gather_fusion.1 = s32[768]{0:T(1024)S(1)} fusion(s32[4096]{0:T(1024)S(1)} %bitcast.1518, s32[1024]{0:T(1024)S(1)} %pad_clamp_fusion.1), kind=kCustom, calls=%fused_computation.1 | custom fusion | bytes 9216 | tf_op jit(solution)/shard_map/gather | solution.py:116
  59.9 4.5 %gather_fusion = s32[768]{0:T(1024)S(1)} fusion(s32[4096]{0:T(1024)S(1)} %bitcast.1517, s32[1024]{0:T(1024)S(1)} %pad_clamp_fusion.2), kind=kCustom, calls=%fused_computation | custom fusion | bytes 9216 | tf_op jit(solution)/shard_map/gather | solution.py:116
  64.4 4.9 %gather_fusion.2 = s32[768]{0:T(1024)S(1)} fusion(s32[4096]{0:T(1024)S(1)} %bitcast.1516, s32[1024]{0:T(1024)S(1)} %pad_clamp_fusion), kind=kCustom, calls=%fused_computation.2 | custom fusion | bytes 9216 | tf_op jit(solution)/shard_map/gather | solution.py:116
  69.4 0.9 compare_and_fusion.6
  70.3 0.9 compare_and_fusion.7
  71.2 0.9 compare_and_fusion.5
  72.1 0.9 compare_and_fusion.4
  73.0 0.9 compare_and_fusion.3
  73.9 0.9 compare_and_fusion.2
  74.8 0.9 compare_and_fusion.1
  75.7 0.9 compare_and_fusion
  81.8 1.5 fusion.48
  83.3 1.3 fusion
  84.6 7.7 %all-gather.14.cloned.1.call-done = bf16[1,1,4096,128]{3,2,1,0:T(8,128)(2,1)} async-done(((bf16[1,1,512,128]{3,2,1,0:T(8,128)(2,1)}), bf16[1,1,4096,128]{3,2,1,0:T(8,128)(2,1)}) %all-gather.14.cloned.1.call-update) | async-done | bytes 1048592 | tf_op jit(solution)/shard_map/all_gather | solution.py:91
  92.3 1.8 fusion.429
  94.3 1.6 fusion.49
  109.4 1.4 fusion.408
  114.0 1.0 copy.220
  115.9 1.0 constant_dynamic-update-slice_fusion.11
  116.9 0.9 constant_dynamic-update-slice_fusion.10
  117.9 0.9 constant_dynamic-update-slice_fusion.9
  118.9 1.3 broadcast_select_fusion.1
  120.2 1.3 collective-permute-start
  122.4 2.0 copy.225
  124.4 5.7 %all-to-all-start.2 = ((bf16[8,3,32,1024]{3,2,1,0:T(8,128)(2,1)}), bf16[8,3,32,1024]{3,2,1,0:T(8,128)(2,1)S(1)}, u32[]{:S(2)}, u32[]{:S(2)}) async-start(bf16[8,3,32,1024]{3,2,1,0:T(8,128)(2,1)} %copy.225), calls=%async_computation.2 | async-start | bytes 3145728 | tf_op jit(solution)/shard_map/all_to_all | solution.py:88
  132.5 2.0 copy.255
  137.7 9.4 %all-to-all-done.2 = bf16[8,3,32,1024]{3,2,1,0:T(8,128)(2,1)S(1)} async-done(((bf16[8,3,32,1024]{3,2,1,0:T(8,128)(2,1)}), bf16[8,3,32,1024]{3,2,1,0:T(8,128)(2,1)S(1)}, u32[]{:S(2)}, u32[]{:S(2)}) %all-to-all-start.2) | async-done | bytes 1572896 | tf_op jit(solution)/shard_map/all_to_all | solution.py:88
  147.0 5.3 %all-to-all-start.3 = ((bf16[8,3,32,1024]{3,2,1,0:T(8,128)(2,1)}), bf16[8,3,32,1024]{3,2,1,0:T(8,128)(2,1)}, u32[]{:S(2)}, u32[]{:S(2)}) async-start(bf16[8,3,32,1024]{3,2,1,0:T(8,128)(2,1)} %copy.255), calls=%async_computation.3 | async-start | bytes 3145728 | tf_op jit(solution)/shard_map/all_to_all | solution.py:88
  152.4 17.3 %collective-permute-done = bf16[8,3,32,1024]{3,2,1,0:T(8,128)(2,1)} collective-permute-done((bf16[8,3,32,1024]{3,2,1,0:T(8,128)(2,1)}, bf16[8,3,32,1024]{3,2,1,0:T(8,128)(2,1)}, u32[]{:S(2)}, u32[]{:S(2)}) %collective-permute-start) | collective-permute-done | bytes 1572896 | tf_op jit(solution)/shard_map/ppermute | solution.py:22
  169.6 2.1 add_convert_fusion.1
  171.7 1.1 fusion.571
  172.9 1.6 fusion.57
  175.1 1.3 fusion.18
  176.4 11.4 %all-gather.18.cloned.1.call-done = bf16[1,1,4096,128]{3,2,1,0:T(8,128)(2,1)} async-done(((bf16[1,1,512,128]{3,2,1,0:T(8,128)(2,1)}), bf16[1,1,4096,128]{3,2,1,0:T(8,128)(2,1)}) %all-gather.18.cloned.1.call-update) | async-done | bytes 1048592 | tf_op jit(solution)/shard_map/all_gather | solution.py:91
  187.8 1.6 fusion.402
  189.6 1.0 copy.293
  194.9 1.7 fusion.399
  198.2 1.7 fusion.396
  202.2 1.7 fusion.393
  206.3 1.7 fusion.390
  210.3 1.7 fusion.387
  214.3 1.7 fusion.384
  217.1 1.3 broadcast_select_fusion
  218.4 1.4 collective-permute-start.1
  230.9 42.0 %collective-permute-done.1 = bf16[8,3,32,1024]{3,2,1,0:T(8,128)(2,1)} collective-permute-done((bf16[8,3,32,1024]{3,2,1,0:T(8,128)(2,1)}, bf16[8,3,32,1024]{3,2,1,0:T(8,128)(2,1)}, u32[]{:S(2)}, u32[]{:S(2)}) %collective-permute-start.1) | collective-permute-done | bytes 1572896 | tf_op jit(solution)/shard_map/ppermute | solution.py:22
  273.0 2.6 add_convert_fusion
  275.6 1.1 fusion.570
  276.8 1.6 fusion.71
  278.9 1.3 fusion.46
  280.2 1.7 fusion.360
  282.1 1.0 copy.307
  291.6 1.7 fusion.372
  294.9 1.7 fusion.375
  298.2 1.7 fusion.378
  302.9 2.3 select_select_fusion.1
  305.2 1.9 maximum_bitcast_fusion
  (491 shorter events, 81.6 us)
Async XLA Ops:
  6.5 13.8 %copy-start.89 = (s32[2,16]{1,0:T(2,128)S(1)}, s32[2,16]{1,0:T(2,128)}, u32[]{:S(2)}) copy-start(s32[2,16]{1,0:T(2,128)} %param.9) | copy-start | bytes 388
  6.5 35.9 %copy-start.3 = (bf16[1,2,512,1024]{3,2,1,0:T(8,128)(2,1)S(1)}, bf16[1,2,512,1024]{3,2,1,0:T(8,128)(2,1)}, u32[]{:S(2)}) copy-start(bf16[1,2,512,1024]{3,2,1,0:T(8,128)(2,1)} %param.5) | copy-start | bytes 6291460
  6.5 75.3 %all-gather.16.cloned.1.call-start = ((), (), s32[]{:S(2)}) async-start(), calls=%async_computation.5 | async-start | bytes 1179648 | tf_op jit(solution)/shard_map/all_gather | solution.py:90
  8.5 83.8 %all-gather.14.cloned.1.call-start = ((), (), s32[]{:S(2)}) async-start(), calls=%async_computation.4 | async-start | bytes 1179648 | tf_op jit(solution)/shard_map/all_gather | solution.py:91
  10.4 162.5 %all-gather.20.cloned.1.call-start = ((), (), s32[]{:S(2)}) async-start(), calls=%async_computation.7 | async-start | bytes 1179648 | tf_op jit(solution)/shard_map/all_gather | solution.py:90
  11.1 176.6 %all-gather.18.cloned.1.call-start = ((), (), s32[]{:S(2)}) async-start(), calls=%async_computation.6 | async-start | bytes 1179648 | tf_op jit(solution)/shard_map/all_gather | solution.py:91
  13.0 37.3 %all-to-all-start = ((s32[8,2,512]{2,1,0:T(2,128)}), s32[8,2,512]{2,1,0:T(2,128)S(1)}, u32[]{:S(2)}, u32[]{:S(2)}) async-start(s32[8,2,512]{2,1,0:T(2,128)} %stack.95), calls=%async_computation | async-start | bytes 65536 | tf_op jit(solution)/shard_map/all_to_all | solution.py:15
  19.8 257.0 %all-gather.24.cloned.1.call-start = ((), (), s32[]{:S(2)}) async-start(), calls=%async_computation.9 | async-start | bytes 1179648 | tf_op jit(solution)/shard_map/all_gather | solution.py:90
  39.2 3.0 copy-start.80
  50.3 26.4 %all-to-all-start.1 = ((bf16[8,3,32,1024]{3,2,1,0:T(8,128)(2,1)}), bf16[8,3,32,1024]{3,2,1,0:T(8,128)(2,1)S(1)}, u32[]{:S(2)}, u32[]{:S(2)}) async-start(bf16[8,3,32,1024]{3,2,1,0:T(8,128)(2,1)} %copy.204), calls=%async_computation.1 | async-start | bytes 3145728 | tf_op jit(solution)/shard_map/all_to_all | solution.py:88
  76.8 5.0 %copy-start.77 = (pred[96,768]{1,0:T(8,128)(4,1)S(1)}, pred[96,768]{1,0:T(8,128)(4,1)}, u32[]{:S(2)}) copy-start(pred[96,768]{1,0:T(8,128)(4,1)} %get-tuple-element.103) | copy-start | bytes 221188
  83.3 9.0 %copy-start.84 = (f32[96,8]{0,1:T(8,128)}, f32[96,8]{0,1:T(8,128)S(1)}, u32[]{:S(2)}) copy-start(f32[96,8]{0,1:T(8,128)S(1)} %get-tuple-element.127) | copy-start | bytes 9220
  94.2 2.4 copy-start.18
  94.3 2.3 copy-start.55
  111.3 5.6 %copy-start.6 = (bf16[96,1,8,128]{3,2,0,1:T(8,128)(2,1)}, bf16[96,1,8,128]{3,2,0,1:T(8,128)(2,1)S(1)}, u32[]{:S(2)}) copy-start(bf16[96,1,8,128]{3,2,0,1:T(8,128)(2,1)S(1)} %copy.212) | copy-start | bytes 589828
  111.5 7.3 %copy-start.8 = (bf16[96,1,8,128]{3,2,0,1:T(8,128)(2,1)}, bf16[96,1,8,128]{3,2,0,1:T(8,128)(2,1)S(1)}, u32[]{:S(2)}) copy-start(bf16[96,1,8,128]{3,2,0,1:T(8,128)(2,1)S(1)} %copy.214) | copy-start | bytes 589828
  112.4 7.8 %copy-start.10 = (bf16[96,1,8,128]{3,2,0,1:T(8,128)(2,1)}, bf16[96,1,8,128]{3,2,0,1:T(8,128)(2,1)S(1)}, u32[]{:S(2)}) copy-start(bf16[96,1,8,128]{3,2,0,1:T(8,128)(2,1)S(1)} %copy.216) | copy-start | bytes 589828
  112.4 6.5 %copy-start.90 = (pred[8,3]{1,0:T(8,128)(4,1)S(1)}, pred[8,3]{1,0:T(8,128)(4,1)}, u32[]{:S(2)}) copy-start(pred[8,3]{1,0:T(8,128)(4,1)} %copy.200) | copy-start | bytes 76
  113.2 7.0 %copy-start.12 = (bf16[96,1,8,128]{3,2,0,1:T(8,128)(2,1)}, bf16[96,1,8,128]{3,2,0,1:T(8,128)(2,1)S(1)}, u32[]{:S(2)}) copy-start(bf16[96,1,8,128]{3,2,0,1:T(8,128)(2,1)S(1)} %copy.218) | copy-start | bytes 589828
  115.0 5.2 %copy-start.14 = (bf16[96,1,8,128]{3,2,0,1:T(8,128)(2,1)}, bf16[96,1,8,128]{3,2,0,1:T(8,128)(2,1)S(1)}, u32[]{:S(2)}) copy-start(bf16[96,1,8,128]{3,2,0,1:T(8,128)(2,1)S(1)} %copy.220) | copy-start | bytes 589828
  115.8 3.0 copy-start.49
  115.9 5.6 %copy-start.5 = (bf16[1,1,512,1024]{3,2,1,0:T(8,128)(2,1)S(1)}, bf16[1,1,512,1024]{3,2,1,0:T(8,128)(2,1)}, u32[]{:S(2)}) copy-start(bf16[1,1,512,1024]{3,2,1,0:T(8,128)(2,1)} %get-tuple-element.13) | copy-start | bytes 3145732
  115.9 5.6 %copy-start.95 = (pred[8,16]{1,0:T(8,128)(4,1)S(1)}, pred[8,16]{1,0:T(8,128)(4,1)}, u32[]{:S(2)}) copy-start(pred[8,16]{1,0:T(8,128)(4,1)} %get-tuple-element.182) | copy-start | bytes 388
  115.9 5.6 %copy-start.98 = (pred[3,16]{1,0:T(4,128)(4,1)S(1)}, pred[3,16]{1,0:T(4,128)(4,1)}, u32[]{:S(2)}) copy-start(pred[3,16]{1,0:T(4,128)(4,1)} %iota_compare_fusion.11) | copy-start | bytes 148
  120.2 49.4 %collective-permute-start = (bf16[8,3,32,1024]{3,2,1,0:T(8,128)(2,1)}, bf16[8,3,32,1024]{3,2,1,0:T(8,128)(2,1)}, u32[]{:S(2)}, u32[]{:S(2)}) collective-permute-start(bf16[8,3,32,1024]{3,2,1,0:T(8,128)(2,1)} %broadcast_select_fusion.1), channel_id=1, source_target_pairs={{0,64},{1,65},{2,66},{3,67},{4,68},{5,69},{6,70},{7,71},{8,72},{9,... | collective-permute-start | bytes 4718600 | tf_op jit(solution)/shard_map/ppermute | solution.py:22
  124.4 6.3 %copy-start.81 = (pred[8,3,16]{2,0,1:T(8,128)(4,1)S(1)}, pred[8,3,16]{2,0,1:T(8,128)(4,1)}, u32[]{:S(2)}) copy-start(pred[8,3,16]{2,0,1:T(8,128)(4,1)} %copy-done.80) | copy-start | bytes 1156
  124.4 6.3 %copy-start.88 = (pred[8,1,16]{2,0,1:T(8,128)(4,1)S(1)}, pred[8,1,16]{2,0,1:T(8,128)(4,1)}, u32[]{:S(2)}) copy-start(pred[8,1,16]{2,0,1:T(8,128)(4,1)} %copy-done.87) | copy-start | bytes 388
  124.4 7.1 %copy-start.97 = (s32[16]{0:T(128)S(1)}, s32[16]{0:T(128)}, u32[]{:S(2)}) copy-start(s32[16]{0:T(128)} %get-tuple-element.179) | copy-start | bytes 196
  124.4 7.1 %copy-start.4 = (bf16[1,1,512,1024]{3,2,1,0:T(8,128)(2,1)S(1)}, bf16[1,1,512,1024]{3,2,1,0:T(8,128)(2,1)}, u32[]{:S(2)}) copy-start(bf16[1,1,512,1024]{3,2,1,0:T(8,128)(2,1)} %get-tuple-element.11) | copy-start | bytes 3145732
  124.4 7.1 %copy-start.94 = (pred[8,16]{1,0:T(8,128)(4,1)S(1)}, pred[8,16]{1,0:T(8,128)(4,1)}, u32[]{:S(2)}) copy-start(pred[8,16]{1,0:T(8,128)(4,1)} %get-tuple-element.181) | copy-start | bytes 388
  124.4 22.6 %all-to-all-start.2 = ((bf16[8,3,32,1024]{3,2,1,0:T(8,128)(2,1)}), bf16[8,3,32,1024]{3,2,1,0:T(8,128)(2,1)S(1)}, u32[]{:S(2)}, u32[]{:S(2)}) async-start(bf16[8,3,32,1024]{3,2,1,0:T(8,128)(2,1)} %copy.225), calls=%async_computation.2 | async-start | bytes 3145728 | tf_op jit(solution)/shard_map/all_to_all | solution.py:88
  130.2 150.0 %all-gather.22.cloned.1.call-start = ((), (), s32[]{:S(2)}) async-start(), calls=%async_computation.8 | async-start | bytes 1179648 | tf_op jit(solution)/shard_map/all_gather | solution.py:91
  131.6 2.9 copy-start.79
  131.6 2.9 copy-start.86
  132.5 3.7 %copy-start.19 = (bf16[96,1,8,128]{3,2,0,1:T(8,128)(2,1)S(1)}, bf16[96,1,8,128]{3,2,0,1:T(8,128)(2,1)}, u32[]{:S(2)}) copy-start(bf16[96,1,8,128]{3,2,0,1:T(8,128)(2,1)} %copy-done.18) | copy-start | bytes 589828
  147.0 83.9 %all-to-all-start.3 = ((bf16[8,3,32,1024]{3,2,1,0:T(8,128)(2,1)}), bf16[8,3,32,1024]{3,2,1,0:T(8,128)(2,1)}, u32[]{:S(2)}, u32[]{:S(2)}) async-start(bf16[8,3,32,1024]{3,2,1,0:T(8,128)(2,1)} %copy.255), calls=%async_computation.3 | async-start | bytes 3145728 | tf_op jit(solution)/shard_map/all_to_all | solution.py:88
  176.4 14.2 %copy-start.1 = (bf16[1,1,4096,128]{3,2,1,0:T(8,128)(2,1)S(1)}, bf16[1,1,4096,128]{3,2,1,0:T(8,128)(2,1)}, u32[]{:S(2)}) copy-start(bf16[1,1,4096,128]{3,2,1,0:T(8,128)(2,1)} %all-gather.20.cloned.1.call-done) | copy-start | bytes 3145732
  176.4 14.2 %copy-start.76 = (pred[96,768]{1,0:T(8,128)(4,1)S(1)}, pred[96,768]{1,0:T(8,128)(4,1)}, u32[]{:S(2)}) copy-start(pred[96,768]{1,0:T(8,128)(4,1)} %get-tuple-element.104) | copy-start | bytes 221188
  189.5 2.3 copy-start.16
  198.2 2.6 copy-start.39
  198.2 2.6 copy-start.66
  202.2 2.6 copy-start.37
  202.2 2.6 copy-start.65
  204.0 2.3 copy-start.26
  206.3 2.6 copy-start.35
  206.3 2.6 copy-start.64
  210.3 2.6 copy-start.33
  210.3 2.6 copy-start.63
  216.3 3.6 %copy-start.44 = (bf16[1,1,3,32,1024]{4,3,2,1,0:T(8,128)(2,1)S(1)}, bf16[1,1,3,32,1024]{4,3,2,1,0:T(8,128)(2,1)}, u32[]{:S(2)}) copy-start(bf16[1,1,3,32,1024]{4,3,2,1,0:T(8,128)(2,1)} %stack.98) | copy-start | bytes 589828
  216.9 3.7 %copy-start.15 = (bf16[96,1,8,128]{3,2,0,1:T(8,128)(2,1)S(1)}, bf16[96,1,8,128]{3,2,0,1:T(8,128)(2,1)}, u32[]{:S(2)}) copy-start(bf16[96,1,8,128]{3,2,0,1:T(8,128)(2,1)} %copy-done.14) | copy-start | bytes 589828
  217.0 3.7 %copy-start.13 = (bf16[96,1,8,128]{3,2,0,1:T(8,128)(2,1)S(1)}, bf16[96,1,8,128]{3,2,0,1:T(8,128)(2,1)}, u32[]{:S(2)}) copy-start(bf16[96,1,8,128]{3,2,0,1:T(8,128)(2,1)} %copy-done.12) | copy-start | bytes 589828
  217.0 3.8 %copy-start.11 = (bf16[96,1,8,128]{3,2,0,1:T(8,128)(2,1)S(1)}, bf16[96,1,8,128]{3,2,0,1:T(8,128)(2,1)}, u32[]{:S(2)}) copy-start(bf16[96,1,8,128]{3,2,0,1:T(8,128)(2,1)} %copy-done.10) | copy-start | bytes 589828
  217.1 3.8 %copy-start.9 = (bf16[96,1,8,128]{3,2,0,1:T(8,128)(2,1)S(1)}, bf16[96,1,8,128]{3,2,0,1:T(8,128)(2,1)}, u32[]{:S(2)}) copy-start(bf16[96,1,8,128]{3,2,0,1:T(8,128)(2,1)} %copy-done.8) | copy-start | bytes 589828
  217.1 3.9 %copy-start.7 = (bf16[96,1,8,128]{3,2,0,1:T(8,128)(2,1)S(1)}, bf16[96,1,8,128]{3,2,0,1:T(8,128)(2,1)}, u32[]{:S(2)}) copy-start(bf16[96,1,8,128]{3,2,0,1:T(8,128)(2,1)} %copy-done.6) | copy-start | bytes 589828
  218.4 6.2 %copy-start.31 = (bf16[96,1,8,128]{3,2,0,1:T(8,128)(2,1)S(1)}, bf16[96,1,8,128]{3,2,0,1:T(8,128)(2,1)}, u32[]{:S(2)}) copy-start(bf16[96,1,8,128]{3,2,0,1:T(8,128)(2,1)} %copy-done.30) | copy-start | bytes 589828
  218.4 54.5 %collective-permute-start.1 = (bf16[8,3,32,1024]{3,2,1,0:T(8,128)(2,1)}, bf16[8,3,32,1024]{3,2,1,0:T(8,128)(2,1)}, u32[]{:S(2)}, u32[]{:S(2)}) collective-permute-start(bf16[8,3,32,1024]{3,2,1,0:T(8,128)(2,1)} %broadcast_select_fusion), channel_id=1, source_target_pairs={{0,64},{1,65},{2,66},{3,67},{4,68},{5,69},{6,70},{7,71},{8,72},{9,... | collective-permute-start | bytes 4718600 | tf_op jit(solution)/shard_map/ppermute | solution.py:22
  220.6 4.2 %copy-start.29 = (bf16[96,1,8,128]{3,2,0,1:T(8,128)(2,1)S(1)}, bf16[96,1,8,128]{3,2,0,1:T(8,128)(2,1)}, u32[]{:S(2)}) copy-start(bf16[96,1,8,128]{3,2,0,1:T(8,128)(2,1)} %copy-done.28) | copy-start | bytes 589828
  220.7 4.2 %copy-start.27 = (bf16[96,1,8,128]{3,2,0,1:T(8,128)(2,1)S(1)}, bf16[96,1,8,128]{3,2,0,1:T(8,128)(2,1)}, u32[]{:S(2)}) copy-start(bf16[96,1,8,128]{3,2,0,1:T(8,128)(2,1)} %copy-done.26) | copy-start | bytes 589828
  220.8 4.2 %copy-start.25 = (bf16[96,1,8,128]{3,2,0,1:T(8,128)(2,1)S(1)}, bf16[96,1,8,128]{3,2,0,1:T(8,128)(2,1)}, u32[]{:S(2)}) copy-start(bf16[96,1,8,128]{3,2,0,1:T(8,128)(2,1)} %copy-done.24) | copy-start | bytes 589828
  220.9 4.2 %copy-start.23 = (bf16[96,1,8,128]{3,2,0,1:T(8,128)(2,1)S(1)}, bf16[96,1,8,128]{3,2,0,1:T(8,128)(2,1)}, u32[]{:S(2)}) copy-start(bf16[96,1,8,128]{3,2,0,1:T(8,128)(2,1)} %copy-done.22) | copy-start | bytes 589828
  221.0 4.2 %copy-start.17 = (bf16[96,1,8,128]{3,2,0,1:T(8,128)(2,1)S(1)}, bf16[96,1,8,128]{3,2,0,1:T(8,128)(2,1)}, u32[]{:S(2)}) copy-start(bf16[96,1,8,128]{3,2,0,1:T(8,128)(2,1)} %copy-done.16) | copy-start | bytes 589828
  221.1 4.2 %copy-start.21 = (bf16[96,1,8,128]{3,2,0,1:T(8,128)(2,1)S(1)}, bf16[96,1,8,128]{3,2,0,1:T(8,128)(2,1)}, u32[]{:S(2)}) copy-start(bf16[96,1,8,128]{3,2,0,1:T(8,128)(2,1)} %copy-done.20) | copy-start | bytes 589828
  280.2 2.9 copy-start
  280.2 2.9 copy-start.61
  (51 other events, 69.4 us)
Sparse Core Ops, SparseCore 0:
  9.0 41.1 all-gather.15
  51.9 40.3 all-gather.13
  93.9 41.7 all-gather.19
  137.2 50.5 all-gather.17
  189.2 38.4 all-gather.23
  229.2 40.2 all-gather.21
